TPU v7x, 512 devices: a whole 4x4x16 slice. The times are simulated.
512 devices in a mesh: seg: 16 (over z_hi, x), coil: 32 (over y, z_lo, core).
Axes of the slice: x: 4, y: 4, z: 16 (z_hi: 4, z_lo: 4; z = z_hi * 4 + z_lo), core: 2. Of those that a mesh axis runs over, the one named last changes fastest.
Arguments:
- image_estimate: bfloat16 [1, 384, 768], replicated, may hold values from -6 to 6
- coil_maps: bfloat16 [32, 384, 768], P('coil'), may hold values from -3 to 3
- field_map: float32 [384, 384], replicated, may hold values from -3 to 3
- interp_rows: bfloat16 [1, 256, 384], replicated, may hold values from -0.3125 to 0.3125
- interp_cols: bfloat16 [1, 128, 384], replicated, may hold values from -0.3125 to 0.3125
- measured: bfloat16 [32, 1, 256, 256], P('coil'), may hold values from -6 to 6
- sample_time: int32 [1, 256], replicated, may hold values from 0 to 60
- sample_count: int32 [1], replicated, may hold values from 128 to 256
Outputs:
- gradient: float32 [1, 384, 768], P(None, 'coil', 'seg')
- residual: float32 [32, 1, 256, 256], P('coil', None, 'seg')
Inputs may be any that keep to these rules, and one draw needn't show every extreme that they name: sample_time counts the sample clock, 4 steps to a segment. Rows below sample_count[p] of partition p are acquired.
All inputs are finite; a program needn't handle non-finite values.
Results may differ from a plain program's by a relative error of at most 0.017.
Values sent between devices are 32-bit elements; how exact they have to be, the bound alone decides.
A program may use at most 64 MiB of HBM per device.

v0:
```python
import math
import jax
import jax.numpy as jnp
from jax import lax
from jax.sharding import PartitionSpec as P

SUBSTEPS = 4


def dft_tables(length):
    indices = jnp.arange(length, dtype=jnp.int32)
    wrapped = indices[:, None] * indices[None, :] % length
    angles = wrapped.astype(jnp.float32) * (2.0 * math.pi / length)
    factor = 1.0 / math.sqrt(length)
    return (jnp.cos(angles) * factor, jnp.sin(angles) * factor)


def shards(
    image_estimate,
    coil_maps,
    field_map,
    interp_rows,
    interp_cols,
    measured,
    sample_time,
    sample_count,
):
    segment = lax.axis_index("seg")
    seg_total = lax.axis_size("seg")
    coil_total = lax.axis_size("coil")
    pixels = field_map.shape[0]
    row_total = interp_rows.shape[1]
    col_total = interp_cols.shape[1]
    own_rows = row_total // seg_total
    start_row = segment * own_rows
    cosine, sine = dft_tables(pixels)
    stacked_table = jnp.concatenate([cosine, sine], axis=0).astype(jnp.bfloat16)
    forward_right = jnp.concatenate(
        [jnp.concatenate([cosine, -sine], 1), jnp.concatenate([sine, cosine], 1)], 0
    ).astype(jnp.bfloat16)
    inverse_right = jnp.concatenate(
        [jnp.concatenate([cosine, sine], 1), jnp.concatenate([-sine, cosine], 1)], 0
    ).astype(jnp.bfloat16)
    offset = segment.astype(jnp.float32) - 0.5 * (seg_total - 1)
    angles = field_map * offset
    phase_re = jnp.cos(angles)
    phase_im = jnp.sin(angles)
    maps = coil_maps[0].astype(jnp.float32)
    sens_re = maps[:, :pixels]
    sens_im = maps[:, pixels:]
    comb_re = sens_re * phase_re - sens_im * phase_im
    comb_im = sens_re * phase_im + sens_im * phase_re
    factor = coil_total ** (-0.5)
    row_ids = jnp.arange(row_total, dtype=jnp.int32)
    current = image_estimate[0].astype(jnp.float32)
    cur_re = current[:, :pixels]
    cur_im = current[:, pixels:]
    weighted = jnp.concatenate(
        [cur_re * comb_re - cur_im * comb_im, cur_re * comb_im + cur_im * comb_re], 1
    ).astype(jnp.bfloat16)
    products = jnp.dot(stacked_table, weighted, preferred_element_type=jnp.float32)
    cos_part = products[:pixels]
    sin_part = products[pixels:]
    rows_ft = jnp.concatenate(
        [cos_part[:, :pixels] + sin_part[:, pixels:], cos_part[:, pixels:] - sin_part[:, :pixels]],
        1,
    ).astype(jnp.bfloat16)
    kspace = jnp.dot(rows_ft, forward_right, preferred_element_type=jnp.float32).astype(
        jnp.bfloat16
    )
    picked = jnp.dot(interp_rows[0], kspace, preferred_element_type=jnp.float32).astype(
        jnp.bfloat16
    )
    sampled = jnp.einsum(
        "mrn,kn->mrk",
        picked.reshape(row_total, 2, pixels),
        interp_cols[0],
        preferred_element_type=jnp.float32,
    ).reshape(row_total, 2 * col_total)
    sample_steps = sample_time[0].astype(jnp.float32)
    weights = jnp.maximum(
        0.0, 1.0 - jnp.abs(sample_steps - (segment * SUBSTEPS).astype(jnp.float32)) / SUBSTEPS
    )
    partial_sum = weights[:, None] * sampled
    sampled_mask = (row_ids < sample_count[0]).astype(jnp.float32)[:, None]
    data_rows = measured[0, 0].astype(jnp.float32)
    totals = lax.psum(partial_sum, "seg")
    misfit = sampled_mask * (totals - data_rows)
    misfit_own = lax.dynamic_slice_in_dim(misfit, start_row, own_rows, 0)
    back_weighted = (weights[:, None] * misfit).astype(jnp.bfloat16)
    spread = lax.dot_general(
        interp_rows[0], back_weighted, (((0,), (0,)), ((), ())), preferred_element_type=jnp.float32
    ).astype(jnp.bfloat16)
    gridded = (
        jnp.einsum(
            "nrk,kj->nrj",
            spread.reshape(pixels, 2, col_total),
            interp_cols[0],
            preferred_element_type=jnp.float32,
        )
        .reshape(pixels, 2 * pixels)
        .astype(jnp.bfloat16)
    )
    back_products = jnp.dot(stacked_table, gridded, preferred_element_type=jnp.float32)
    cos_back = back_products[:pixels]
    sin_back = back_products[pixels:]
    back_rows = jnp.concatenate(
        [cos_back[:, :pixels] - sin_back[:, pixels:], cos_back[:, pixels:] + sin_back[:, :pixels]],
        1,
    ).astype(jnp.bfloat16)
    back_image = jnp.dot(back_rows, inverse_right, preferred_element_type=jnp.float32)
    image_re = back_image[:, :pixels]
    image_im = back_image[:, pixels:]
    image_term = factor * jnp.concatenate(
        [comb_re * image_re + comb_im * image_im, comb_re * image_im - comb_im * image_re], 1
    )
    across = lax.psum_scatter(image_term, "coil", scatter_dimension=0, tiled=True)
    reduced = lax.psum_scatter(across, "seg", scatter_dimension=1, tiled=True)
    gradients = [reduced]
    residuals = [misfit_own]
    gradient = jnp.stack(gradients, axis=0)
    residual = jnp.stack(residuals, axis=0)[None]
    return (gradient, residual)


def solution(mesh):
    in_specs = (P(), P("coil", None, None), P(), P(), P(), P("coil", None, None, None), P(), P())
    out_specs = (P(None, "coil", "seg"), P("coil", None, "seg", None))
    return jax.shard_map(shards, mesh=mesh, in_specs=in_specs, out_specs=out_specs, check_vma=False)
```

profile of v0, /device:TPU:8, one launch (start us, length us, event | category | flops | bytes accessed | tf_op | source)
XLA Modules:
  0.0 456.2 jit_solution(10161998638075263033)
XLA Ops:
  7.2 0.0 copy-start
  7.2 0.0 all-reduce.4.cloned.1.call-start
  7.2 3.0 negate_convert_fusion
  10.2 2.6 multiply_convert_fusion
  12.8 0.0 copy-start.1
  12.8 1.3 bitcast_convert_fusion
  14.1 2.4 subtract_convert_fusion
  16.5 0.2 add_convert_fusion
  16.7 0.8 fusion.21
  17.5 0.1 fusion.20
  17.6 0.0 copy-start.3
  17.6 2.3 fusion.2
  19.9 0.0 copy-start.6
  20.0 0.2 fusion.44
  20.2 0.1 copy.16
  20.3 0.3 copy-done.6
  20.6 0.8 broadcast_multiply_fusion
  21.4 0.0 all-reduce.4.cloned.1.call-update
  21.4 0.0 reduce-scatter.6.cloned.1.call-start
  22.2 205.4 %all-reduce.4.cloned.1.call-done = f32[256,256]{1,0:T(8,128)} async-done(((f32[256,256]{1,0:T(8,128)}), f32[256,256]{1,0:T(8,128)}) %all-reduce.4.cloned.1.call-update) | async-done | bytes 262160 | tf_op jit(solution)/shard_map/psum | solution.py:87
  227.6 1.0 fusion.39
  228.7 0.3 convolution_convert_fusion.2
  229.0 0.4 convolution_convert_fusion
  229.4 0.8 fusion.38
  230.2 0.1 fusion.18
  230.3 0.8 copy-done.4
  231.1 0.7 fusion.7
  231.8 0.2 multiply_add_fusion
  232.0 0.1 maximum_multiply_fusion
  232.1 67.6 %fusion = f32[16,768]{1,0:T(8,128)S(1)} fusion(f32[384,768]{1,0:T(8,128)S(1)} %maximum_multiply_fusion), kind=kCustom, calls=%all-reduce-scatter | all-reduce-scatter fusion | flops 393217 | bytes 1230848
  299.8 1.9 collective-permute-start.6
  301.7 1.9 collective-permute-start.5
  303.6 8.6 %collective-permute-start.7 = (f32[12,768]{1,0:T(8,128)S(1)}, f32[12,768]{1,0:T(8,128)S(1)}, u32[]{:S(2)}, u32[]{:S(2)}) collective-permute-start(f32[12,768]{1,0:T(8,128)S(1)} %slice.82), channel_id=1, source_target_pairs={{0,8},{1,9},{2,10},{3,11},{4,12},{5,13},{6,14},{7,15},{8,16},{9,17... | collective-permute-start | bytes 110600
  312.2 1.9 collective-permute-start.4
  314.2 8.2 %collective-permute-start.3 = (f32[16,768]{1,0:T(8,128)S(1)}, f32[16,768]{1,0:T(8,128)S(1)}, u32[]{:S(2)}, u32[]{:S(2)}) collective-permute-start(f32[16,768]{1,0:T(8,128)S(1)} %fusion), channel_id=1, source_target_pairs={{0,4},{1,5},{2,6},{3,7},{4,8},{5,9},{6,10},{7,11},{8,12},{9,13},{1... | collective-permute-start | bytes 147464
  322.4 1.9 collective-permute-start.2
  324.3 3.4 collective-permute-start.1
  327.7 2.9 collective-permute-start
  330.7 1.3 dynamic-slice.4
  332.6 1.3 collective-permute-done.1
  333.9 2.0 collective-permute-done
  335.8 1.0 concatenate.54
  336.9 0.9 copy.24
  337.8 0.0 reduce-scatter.6.cloned.1.call-update
  337.8 0.6 dynamic-slice_bitcast_fusion
  338.5 109.4 %reduce-scatter.6.cloned.1.call-done = f32[48,12]{1,0:T(8,128)} async-done(((f32[768,12]{1,0:T(8,128)}), f32[48,12]{1,0:T(8,128)}) %reduce-scatter.6.cloned.1.call-update) | async-done | bytes 2320
  447.9 0.8 copy.25
  448.7 0.6 copy.19
  (18 shorter events, 0.1 us)
Async XLA Ops:
  7.2 10.5 %copy-start = (bf16[1,256,384]{2,1,0:T(8,128)(2,1)S(1)}, bf16[1,256,384]{2,1,0:T(8,128)(2,1)}, u32[]{:S(2)}) copy-start(bf16[1,256,384]{2,1,0:T(8,128)(2,1)} %param.11) | copy-start | bytes 589828
  7.2 5.6 %copy-start.2 = (bf16[1,384,768]{2,1,0:T(8,128)(2,1)S(1)}, bf16[1,384,768]{2,1,0:T(8,128)(2,1)}, u32[]{:S(2)}) copy-start(bf16[1,384,768]{2,1,0:T(8,128)(2,1)} %param.8) | copy-start | bytes 1769476
  7.2 220.4 %all-reduce.4.cloned.1.call-start = ((), (), s32[]{:S(2)}) async-start(), calls=%async_computation.1 | async-start | bytes 524288 | tf_op jit(solution)/shard_map/psum | solution.py:87
  12.8 1.3 copy-start.1
  17.6 2.3 copy-start.3
  19.9 0.7 copy-start.6
  19.9 207.7 %copy-start.5 = (bf16[1,1,256,256]{3,2,1,0:T(8,128)(2,1)S(1)}, bf16[1,1,256,256]{3,2,1,0:T(8,128)(2,1)}, u32[]{:S(2)}) copy-start(bf16[1,1,256,256]{3,2,1,0:T(8,128)(2,1)} %param.13) | copy-start | bytes 393220
  21.4 426.5 %reduce-scatter.6.cloned.1.call-start = ((), (), s32[]{:S(2)}) async-start(), calls=%async_computation.2 | async-start | bytes 417792
  230.2 1.0 copy-start.4
  299.8 24.6 %collective-permute-start.6 = (f32[16,768]{1,0:T(8,128)S(1)}, f32[16,768]{1,0:T(8,128)S(1)}, u32[]{:S(2)}, u32[]{:S(2)}) collective-permute-start(f32[16,768]{1,0:T(8,128)S(1)} %fusion), channel_id=1, source_target_pairs={{0,7},{1,8},{2,9},{3,10},{4,11},{5,12},{6,13},{7,14},{8,15},{9,16}... | collective-permute-start | bytes 147464
  301.7 26.0 %collective-permute-start.5 = (f32[16,768]{1,0:T(8,128)S(1)}, f32[16,768]{1,0:T(8,128)S(1)}, u32[]{:S(2)}, u32[]{:S(2)}) collective-permute-start(f32[16,768]{1,0:T(8,128)S(1)} %fusion), channel_id=1, source_target_pairs={{0,6},{1,7},{2,8},{3,9},{4,10},{5,11},{6,12},{7,13},{8,14},{9,15},... | collective-permute-start | bytes 147464
  303.6 18.7 %collective-permute-start.7 = (f32[12,768]{1,0:T(8,128)S(1)}, f32[12,768]{1,0:T(8,128)S(1)}, u32[]{:S(2)}, u32[]{:S(2)}) collective-permute-start(f32[12,768]{1,0:T(8,128)S(1)} %slice.82), channel_id=1, source_target_pairs={{0,8},{1,9},{2,10},{3,11},{4,12},{5,13},{6,14},{7,15},{8,16},{9,17... | collective-permute-start | bytes 110600
  312.2 20.3 %collective-permute-start.4 = (f32[16,768]{1,0:T(8,128)S(1)}, f32[16,768]{1,0:T(8,128)S(1)}, u32[]{:S(2)}, u32[]{:S(2)}) collective-permute-start(f32[16,768]{1,0:T(8,128)S(1)} %fusion), channel_id=1, source_target_pairs={{0,5},{1,6},{2,7},{3,8},{4,9},{5,10},{6,11},{7,12},{8,13},{9,14},{... | collective-permute-start | bytes 147464
  314.2 18.4 %collective-permute-start.3 = (f32[16,768]{1,0:T(8,128)S(1)}, f32[16,768]{1,0:T(8,128)S(1)}, u32[]{:S(2)}, u32[]{:S(2)}) collective-permute-start(f32[16,768]{1,0:T(8,128)S(1)} %fusion), channel_id=1, source_target_pairs={{0,4},{1,5},{2,6},{3,7},{4,8},{5,9},{6,10},{7,11},{8,12},{9,13},{1... | collective-permute-start | bytes 147464
  322.4 10.2 %collective-permute-start.2 = (f32[16,768]{1,0:T(8,128)S(1)}, f32[16,768]{1,0:T(8,128)S(1)}, u32[]{:S(2)}, u32[]{:S(2)}) collective-permute-start(f32[16,768]{1,0:T(8,128)S(1)} %fusion), channel_id=1, source_target_pairs={{0,3},{1,4},{2,5},{3,6},{4,7},{5,8},{6,9},{7,10},{8,11},{9,12},{10... | collective-permute-start | bytes 147464
  324.3 9.5 %collective-permute-start.1 = (f32[16,768]{1,0:T(8,128)S(1)}, f32[16,768]{1,0:T(8,128)S(1)}, u32[]{:S(2)}, u32[]{:S(2)}) collective-permute-start(f32[16,768]{1,0:T(8,128)S(1)} %fusion), channel_id=1, source_target_pairs={{0,2},{1,3},{2,4},{3,5},{4,6},{5,7},{6,8},{7,9},{8,10},{9,11},{10,... | collective-permute-start | bytes 147464
  327.7 8.1 %collective-permute-start = (f32[16,768]{1,0:T(8,128)S(1)}, f32[16,768]{1,0:T(8,128)S(1)}, u32[]{:S(2)}, u32[]{:S(2)}) collective-permute-start(f32[16,768]{1,0:T(8,128)S(1)} %fusion), channel_id=1, source_target_pairs={{0,1},{1,2},{2,3},{3,4},{4,5},{5,6},{6,7},{7,8},{8,9},{9,10},{10,1... | collective-permute-start | bytes 147464
Sparse Core Ops, SparseCore 0:
  21.6 205.9 all-reduce.3
  338.0 109.8 reduce-scatter.5
where the time goes:
time: 457 us; the launch traced here: 456 us
  waiting for transfers between devices  318 us (70%)
  blocking collectives  67.6 us (15%)
  starting transfers between devices  30.9 us (7%)
  between operations  15.7 us (3%)
  other arithmetic  11.7 us (3%)
  local copies, waits for them, and re-layouts  6.57 us (1%)
  matrix products  5.5 us (1%)
    psum x1, waiting for transfers between devices, shards(): totals = lax.psum(partial_sum, 'seg')  205 us
    unnamed x11, waiting for transfers between devices  113 us
    unnamed x1, blocking collectives  67.6 us
    unnamed x9, starting transfers between devices  30.8 us
  transfers between devices with their start and end apart: 10, of which 4 were waited for; matrix products, arithmetic and copies ran while one was open for 0% of the time, Pallas kernels for 0%

commit v1 on v0

--- a/solution.py
+++ b/solution.py
@@ -84,7 +84,8 @@
     partial_sum = weights[:, None] * sampled
     sampled_mask = (row_ids < sample_count[0]).astype(jnp.float32)[:, None]
     data_rows = measured[0, 0].astype(jnp.float32)
-    totals = lax.psum(partial_sum, "seg")
+    parts = lax.all_gather(partial_sum, "seg")
+    totals = jnp.sum(parts, axis=0)
     misfit = sampled_mask * (totals - data_rows)
     misfit_own = lax.dynamic_slice_in_dim(misfit, start_row, own_rows, 0)
     back_weighted = (weights[:, None] * misfit).astype(jnp.bfloat16)

time: 457 us -> 384 us (0.84)
  waiting for transfers between devices: 318 us -> 246 us
    psum x1 -> x0, waiting for transfers between devices: 205 us -> none  [shards(): totals = lax.psum(partial_sum, 'seg')]
    all_gather x0 -> x1, waiting for transfers between devices: none -> 138 us  [shards(): parts = lax.all_gather(partial_sum, 'seg')]
  transfers between devices with their start and end apart: 10 -> 10, of which waited for: 4 -> 5; matrix products, arithmetic and copies ran while one was open for 0% -> 1% of each run, Pallas kernels for 0% -> 0%
where the time goes in v1:
time: 384 us
  waiting for transfers between devices  246 us (64%)
  blocking collectives  66.4 us (17%)
  starting transfers between devices  27.4 us (7%)
  other arithmetic  15.8 us (4%)
  between operations  15.7 us (4%)
  local copies, waits for them, and re-layouts  6.92 us (2%)
  matrix products  5.4 us (1%)
    all_gather x1, waiting for transfers between devices, shards(): parts = lax.all_gather(partial_sum, 'seg')  138 us
    unnamed x11, waiting for transfers between devices  108 us
    unnamed x1, blocking collectives  66.4 us
    unnamed x9, starting transfers between devices  27.4 us
    another operation x6, other arithmetic  9.78 us
  transfers between devices with their start and end apart: 10, of which 5 were waited for; matrix products, arithmetic and copies ran while one was open for 1% of the time, Pallas kernels for 0%

profile of v1, /device:TPU:8, one launch (start us, length us, event | category | flops | bytes accessed | tf_op | source)
XLA Modules:
  0.0 383.8 jit_solution(2147771669760490195)
XLA Ops:
  7.2 0.0 all-gather.2.cloned.1.call-start
  7.2 2.6 multiply_convert_fusion
  9.8 3.0 negate_convert_fusion
  12.8 2.3 bitcast_convert_fusion
  15.1 3.9 %subtract_convert_fusion = (bf16[384,384]{1,0:T(8,128)(2,1)S(1)}, f32[384,384]{1,0:T(8,128)S(1)}, f32[384,384]{1,0:T(8,128)S(1)}) fusion(f32[384,768]{1,0:T(8,128)S(1)} %get-tuple-element.17, f32[384,768]{1,0:T(8,128)} %get-tuple-element.18, f32[384,384]{1,0:T(8,128)} %param.10, f32[]{:T(128)S(6)} %sub.45), kind=kLoop, calls=%fused_computation.45 | loop fusion | flops 1622016 | bytes 4423684 | tf_op jit(solution)/shard_map/convert.19
  19.0 0.1 add_convert_fusion
  19.1 0.8 fusion.21
  19.9 0.1 fusion.20
  20.1 2.3 fusion.2
  22.4 0.2 fusion.50
  22.6 0.1 copy.22
  22.8 0.3 copy-done.5
  23.0 0.8 broadcast_multiply_fusion
  23.8 0.0 all-gather.2.cloned.1.call-update
  23.9 0.0 reduce-scatter.6.cloned.1.call-start
  23.9 0.1 copy.24
  24.7 137.8 %all-gather.2.cloned.1.call-done = f32[16,256,256]{2,1,0:T(8,128)} async-done(((f32[1,256,256]{2,1,0:T(8,128)}), f32[16,256,256]{2,1,0:T(8,128)}) %all-gather.2.cloned.1.call-update) | async-done | bytes 4194320 | tf_op jit(solution)/shard_map/all_gather | solution.py:87
  162.5 2.5 reduce_sum.11
  165.0 0.1 copy.35
  165.2 0.2 convolution_convert_fusion.2
  165.4 0.4 convolution_convert_fusion
  165.8 0.8 fusion.38
  166.6 0.1 fusion.18
  166.7 0.8 copy-done.3
  167.5 0.7 fusion.7
  168.2 0.2 multiply_add_fusion
  168.4 0.1 maximum_multiply_fusion
  168.5 66.4 %fusion = f32[16,768]{1,0:T(8,128)S(1)} fusion(f32[384,768]{1,0:T(8,128)S(1)} %maximum_multiply_fusion), kind=kCustom, calls=%all-reduce-scatter | all-reduce-scatter fusion | flops 393217 | bytes 1230848
  234.9 1.9 collective-permute-start
  236.8 1.9 collective-permute-start.1
  238.7 3.4 collective-permute-start.7
  242.2 1.9 collective-permute-start.2
  244.1 6.7 %collective-permute-start.3 = (f32[16,768]{1,0:T(8,128)S(1)}, f32[16,768]{1,0:T(8,128)S(1)}, u32[]{:S(2)}, u32[]{:S(2)}) collective-permute-start(f32[16,768]{1,0:T(8,128)S(1)} %fusion), channel_id=1, source_target_pairs={{0,4},{1,5},{2,6},{3,7},{4,8},{5,9},{6,10},{7,11},{8,12},{9,13},{1... | collective-permute-start | bytes 147464
  250.8 2.8 collective-permute-done.7
  253.6 7.7 %collective-permute-start.4 = (f32[16,768]{1,0:T(8,128)S(1)}, f32[16,768]{1,0:T(8,128)S(1)}, u32[]{:S(2)}, u32[]{:S(2)}) collective-permute-start(f32[16,768]{1,0:T(8,128)S(1)} %fusion), channel_id=1, source_target_pairs={{0,5},{1,6},{2,7},{3,8},{4,9},{5,10},{6,11},{7,12},{8,13},{9,14},{... | collective-permute-start | bytes 147464
  261.3 1.9 collective-permute-start.5
  263.3 1.9 collective-permute-start.6
  265.2 0.1 dynamic-slice.2
  265.3 1.3 dynamic-slice.5
  267.2 1.0 collective-permute-done.5
  268.2 0.5 collective-permute-done.6
  268.7 1.0 concatenate.54
  269.8 0.9 copy.33
  270.7 0.1 fusion.46
  270.9 0.7 copy.27
  271.6 104.0 %reduce-scatter.6.cloned.1.call-done = f32[48,12]{1,0:T(8,128)} async-done(((f32[768,12]{1,0:T(8,128)}), f32[48,12]{1,0:T(8,128)}) %reduce-scatter.6.cloned.1.call-update) | async-done | bytes 2320
  375.6 0.8 copy.34
  376.4 0.6 copy.28
  (21 shorter events, 0.1 us)
Async XLA Ops:
  7.2 12.9 %copy-start = (bf16[1,256,384]{2,1,0:T(8,128)(2,1)S(1)}, bf16[1,256,384]{2,1,0:T(8,128)(2,1)}, u32[]{:S(2)}) copy-start(bf16[1,256,384]{2,1,0:T(8,128)(2,1)} %param.11) | copy-start | bytes 589828
  7.2 5.6 %copy-start.1 = (bf16[1,384,768]{2,1,0:T(8,128)(2,1)S(1)}, bf16[1,384,768]{2,1,0:T(8,128)(2,1)}, u32[]{:S(2)}) copy-start(bf16[1,384,768]{2,1,0:T(8,128)(2,1)} %param.8) | copy-start | bytes 1769476
  7.2 155.3 %all-gather.2.cloned.1.call-start = ((), (), s32[]{:S(2)}) async-start(), calls=%async_computation.1 | async-start | bytes 4456448 | tf_op jit(solution)/shard_map/all_gather | solution.py:87
  20.1 2.3 copy-start.2
  22.3 0.7 copy-start.5
  22.4 1.6 copy-start.4
  23.9 351.7 %reduce-scatter.6.cloned.1.call-start = ((), (), s32[]{:S(2)}) async-start(), calls=%async_computation.2 | async-start | bytes 417792
  166.6 1.0 copy-start.3
  234.9 26.4 %collective-permute-start = (f32[16,768]{1,0:T(8,128)S(1)}, f32[16,768]{1,0:T(8,128)S(1)}, u32[]{:S(2)}, u32[]{:S(2)}) collective-permute-start(f32[16,768]{1,0:T(8,128)S(1)} %fusion), channel_id=1, source_target_pairs={{0,1},{1,2},{2,3},{3,4},{4,5},{5,6},{6,7},{7,8},{8,9},{9,10},{10,1... | collective-permute-start | bytes 147464
  236.8 26.4 %collective-permute-start.1 = (f32[16,768]{1,0:T(8,128)S(1)}, f32[16,768]{1,0:T(8,128)S(1)}, u32[]{:S(2)}, u32[]{:S(2)}) collective-permute-start(f32[16,768]{1,0:T(8,128)S(1)} %fusion), channel_id=1, source_target_pairs={{0,2},{1,3},{2,4},{3,5},{4,6},{5,7},{6,8},{7,9},{8,10},{9,11},{10,... | collective-permute-start | bytes 147464
  238.7 14.9 %collective-permute-start.7 = (f32[12,768]{1,0:T(8,128)S(1)}, f32[12,768]{1,0:T(8,128)S(1)}, u32[]{:S(2)}, u32[]{:S(2)}) collective-permute-start(f32[12,768]{1,0:T(8,128)S(1)} %slice.82), channel_id=1, source_target_pairs={{0,8},{1,9},{2,10},{3,11},{4,12},{5,13},{6,14},{7,15},{8,16},{9,17... | collective-permute-start | bytes 110600
  242.2 25.0 %collective-permute-start.2 = (f32[16,768]{1,0:T(8,128)S(1)}, f32[16,768]{1,0:T(8,128)S(1)}, u32[]{:S(2)}, u32[]{:S(2)}) collective-permute-start(f32[16,768]{1,0:T(8,128)S(1)} %fusion), channel_id=1, source_target_pairs={{0,3},{1,4},{2,5},{3,6},{4,7},{5,8},{6,9},{7,10},{8,11},{9,12},{10... | collective-permute-start | bytes 147464
  244.1 23.1 %collective-permute-start.3 = (f32[16,768]{1,0:T(8,128)S(1)}, f32[16,768]{1,0:T(8,128)S(1)}, u32[]{:S(2)}, u32[]{:S(2)}) collective-permute-start(f32[16,768]{1,0:T(8,128)S(1)} %fusion), channel_id=1, source_target_pairs={{0,4},{1,5},{2,6},{3,7},{4,8},{5,9},{6,10},{7,11},{8,12},{9,13},{1... | collective-permute-start | bytes 147464
  253.6 13.6 %collective-permute-start.4 = (f32[16,768]{1,0:T(8,128)S(1)}, f32[16,768]{1,0:T(8,128)S(1)}, u32[]{:S(2)}, u32[]{:S(2)}) collective-permute-start(f32[16,768]{1,0:T(8,128)S(1)} %fusion), channel_id=1, source_target_pairs={{0,5},{1,6},{2,7},{3,8},{4,9},{5,10},{6,11},{7,12},{8,13},{9,14},{... | collective-permute-start | bytes 147464
  261.3 6.9 %collective-permute-start.5 = (f32[16,768]{1,0:T(8,128)S(1)}, f32[16,768]{1,0:T(8,128)S(1)}, u32[]{:S(2)}, u32[]{:S(2)}) collective-permute-start(f32[16,768]{1,0:T(8,128)S(1)} %fusion), channel_id=1, source_target_pairs={{0,6},{1,7},{2,8},{3,9},{4,10},{5,11},{6,12},{7,13},{8,14},{9,15},... | collective-permute-start | bytes 147464
  263.3 5.5 %collective-permute-start.6 = (f32[16,768]{1,0:T(8,128)S(1)}, f32[16,768]{1,0:T(8,128)S(1)}, u32[]{:S(2)}, u32[]{:S(2)}) collective-permute-start(f32[16,768]{1,0:T(8,128)S(1)} %fusion), channel_id=1, source_target_pairs={{0,7},{1,8},{2,9},{3,10},{4,11},{5,12},{6,13},{7,14},{8,15},{9,16}... | collective-permute-start | bytes 147464
Sparse Core Ops, SparseCore 0:
  24.0 138.5 all-gather.1
  270.9 104.6 reduce-scatter.5
